TPU v7x, 32 devices: a whole 2x2x4 slice. The times are simulated.
32 devices in a mesh: row: 4 (over x, core), col: 8 (over z, y).
Axes of the slice: x: 2, y: 2, z: 4, core: 2. Of those that a mesh axis runs over, the one named last changes fastest.
Arguments:
- act_values: bfloat16 [512, 16384], P('col', 'row'), may hold values from -6 to 6
- act_scales: float32 [512, 128], P('col', 'row'), may hold values from 0.3 to 4
- grad_values: bfloat16 [512, 28672], P('row', 'col'), may hold values from -6 to 6
- grad_scales: float32 [512, 224], P('row', 'col'), may hold values from 0.3 to 4
- weight: bfloat16 [16384, 28672], P('row', 'col'), may hold values from -0.03125 to 0.03125
Outputs:
- input_grad: bfloat16 [512, 16384], P('col', 'row')
- weight_grad: bfloat16 [16384, 28672], P('row', 'col')
All inputs are finite; a program needn't handle non-finite values.
Results may differ from a plain program's by a relative error of at most 0.015.
Values may be sent and summed in bfloat16 or wider, within the bound.
A program may use at most 128 MiB of HBM per device.

v0:
```python
import jax
import jax.numpy as jnp
from jax import lax
from jax.sharding import PartitionSpec as P

QB = 128


def dequantize(values, scales):
    height, breadth = values.shape
    scaled = values.astype(jnp.float32).reshape(height, breadth // QB, QB) * scales[:, :, None]
    return scaled.reshape(height, breadth).astype(jnp.bfloat16)


def shards(act_values, act_scales, grad_values, grad_scales, weight):
    act_local = dequantize(act_values, act_scales)
    grad_local = dequantize(grad_values, grad_scales)
    activations = lax.all_gather(act_local, "col", axis=0, tiled=True)
    gradients = lax.all_gather(grad_local, "row", axis=0, tiled=True)
    weight_grad = lax.dot_general(
        activations, gradients, (((0,), (0,)), ((), ())), preferred_element_type=jnp.float32
    ).astype(jnp.bfloat16)
    summed = lax.psum_scatter(
        lax.dot_general(
            gradients, weight, (((1,), (1,)), ((), ())), preferred_element_type=jnp.float32
        ).astype(jnp.bfloat16),
        "col",
        scatter_dimension=0,
        tiled=True,
    )
    return (summed, weight_grad)


def solution(mesh):
    placed = (P("col", "row"), P("col", "row"), P("row", "col"), P("row", "col"), P("row", "col"))
    return jax.shard_map(
        shards,
        mesh=mesh,
        in_specs=placed,
        out_specs=(P("col", "row"), P("row", "col")),
        check_vma=False,
    )
```

profile of v0, /device:TPU:0, one launch (start us, length us, event | category | flops | bytes accessed | tf_op | source)
XLA Modules:
  0.0 218.0 jit_solution(4168408366819208629)
XLA Ops:
  7.2 0.0 copy-start.1
  7.2 0.0 copy-start
  7.2 0.0 all-gather.3.cloned.1.call-start
  7.2 1.6 copy.9
  8.8 1.8 fusion
  10.7 0.0 all-gather.3.cloned.1.call-update
  10.7 0.0 all-gather.5.cloned.1.call-start
  10.7 0.0 copy-done.1
  10.7 0.1 copy.10
  10.8 0.3 mul.25
  11.2 0.0 copy-done
  11.2 1.4 fusion.1
  12.6 0.0 all-gather.5.cloned.1.call-update
  12.6 0.0 reduce-scatter.2.cloned.1.call-start
  12.7 32.9 %all-gather.3.cloned.1.call-done = bf16[512,3584]{0,1:T(8,128)(2,1)} async-done(((bf16[128,3584]{0,1:T(8,128)(2,1)}), bf16[512,3584]{0,1:T(8,128)(2,1)}) %all-gather.3.cloned.1.call-update) | async-done | bytes 3670032 | tf_op jit(solution)/shard_map/all_gather | solution.py:19
  45.5 23.8 %convolution_convert_fusion.1 = bf16[512,4096]{1,0:T(8,128)(2,1)} fusion(bf16[512,3584]{0,1:T(8,128)(2,1)} %all-gather.3.cloned.1.call-done, bf16[4096,3584]{1,0:T(8,128)(2,1)} %param.9), kind=kOutput, calls=%fused_computation.1 | convolution fusion | flops 15034482688 | bytes 37224448 | tf_op jit(solution)/shard_map/dot_general | solution.py:24
  69.3 0.0 reduce-scatter.2.cloned.1.call-update
  69.3 51.7 %all-gather.5.cloned.1.call-done = bf16[512,4096]{1,0:T(8,128)(2,1)} async-done(((bf16[64,4096]{1,0:T(8,128)(2,1)}), bf16[512,4096]{1,0:T(8,128)(2,1)}) %all-gather.5.cloned.1.call-update) | async-done | bytes 4194320 | tf_op jit(solution)/shard_map/all_gather | solution.py:18
  121.1 22.6 %convolution_convert_fusion = bf16[4096,3584]{1,0:T(8,128)(2,1)} fusion(bf16[512,4096]{1,0:T(8,128)(2,1)} %all-gather.5.cloned.1.call-done, bf16[512,3584]{0,1:T(8,128)(2,1)} %all-gather.3.cloned.1.call-done), kind=kOutput, calls=%fused_computation | convolution fusion | flops 15047065600 | bytes 37224448 | tf_op jit(solution)/shard_map/dot_general | solution.py:20
  143.7 67.8 %reduce-scatter.2.cloned.1.call-done = bf16[64,4096]{1,0:T(8,128)(2,1)} async-done(((bf16[512,4096]{1,0:T(8,128)(2,1)}), bf16[64,4096]{1,0:T(8,128)(2,1)}) %reduce-scatter.2.cloned.1.call-update) | async-done | bytes 524304 | tf_op jit(solution)/shard_map/reduce_scatter | solution.py:23
Async XLA Ops:
  7.2 3.6 %copy-start.1 = (f32[64,32]{0,1:T(8,128)S(1)}, f32[64,32]{0,1:T(8,128)}, u32[]{:S(2)}) copy-start(f32[64,32]{0,1:T(8,128)} %param.6) | copy-start | bytes 24580
  7.2 4.0 %copy-start = (bf16[64,4096]{1,0:T(8,128)(2,1)S(1)}, bf16[64,4096]{1,0:T(8,128)(2,1)}, u32[]{:S(2)}) copy-start(bf16[64,4096]{1,0:T(8,128)(2,1)} %param.5) | copy-start | bytes 1572868
  7.2 38.3 %all-gather.3.cloned.1.call-start = ((), (), s32[]{:S(2)}) async-start(), calls=%async_computation.1 | async-start | bytes 4587520 | tf_op jit(solution)/shard_map/all_gather | solution.py:19
  10.7 110.4 %all-gather.5.cloned.1.call-start = ((), (), s32[]{:S(2)}) async-start(), calls=%async_computation.3 | async-start | bytes 4718592 | tf_op jit(solution)/shard_map/all_gather | solution.py:18
  12.6 198.9 %reduce-scatter.2.cloned.1.call-start = ((), (), s32[]{:S(2)}) async-start(), calls=%async_computation.2 | async-start | bytes 4718592 | tf_op jit(solution)/shard_map/reduce_scatter | solution.py:23
Sparse Core Ops, SparseCore 0:
  10.8 34.6 all-gather.2
  47.6 73.3 all-gather.4
  125.3 86.1 reduce-scatter.1
where the time goes:
time: 218 us
  waiting for transfers between devices  152 us (70%)
  matrix products  46.4 us (21%)
  between operations  13.8 us (6%)
  other arithmetic  3.23 us (1%)
    reduce_scatter x1, waiting for transfers between devices, shards(): lax.psum_scatter(lax.dot_general(gradients, weight, (((1,), (1,)), ((), (...  67.8 us
    all_gather x1, waiting for transfers between devices, shards(): activations = lax.all_gather(act_local, 'col', axis=0, tiled=True)  51.7 us
    all_gather x1, waiting for transfers between devices, shards(): gradients = lax.all_gather(grad_local, 'row', axis=0, tiled=True)  32.9 us
    dot_general x1, matrix products, shards(): lax.dot_general(gradients, weight, (((1,), (1,)), ((), ())), preferred_el...  23.8 us
    dot_general x1, matrix products, shards(): lax.dot_general(activations, gradients, (((0,), (0,)), ((), ())), preferr...  22.6 us
  transfers between devices with their start and end apart: 3, of which 3 were waited for; matrix products, arithmetic and copies ran while one was open for 22% of the time, Pallas kernels for 0%

commit v1 on v0

v1 whole, which is shorter than its diff:
```python
import functools

import jax
import jax.numpy as jnp
from jax import lax
from jax.experimental import pallas as pl
from jax.experimental.pallas import tpu as pltpu
from jax.sharding import PartitionSpec as P

QB = 128
PIECES = 4
SUBS = 2
LATE = 3
MESH = pl.DeviceIdType.MESH


def kernel(n_row, n_col, act_v, act_s, grad_v, grad_s, weight, out, act_all, grad_all,
           own, grads, wv, part, got, ag_send, ag_recv, rs_send, rs_recv,
           g_send, g_recv, w_sem, local_sem):
    row, col = lax.axis_index("row"), lax.axis_index("col")
    n_x, n_z = n_row // 2, n_col // 2
    core, x = row % 2, row // 2
    tb, width = act_v.shape
    half = width // 2
    sub = half // SUBS
    piece = half // PIECES
    tr = grad_v.shape[0]

    def to_col(q):
        q = lax.rem(q + 2 * n_col, n_col)
        back = q // n_z
        return (1 - back) * 2 * q + back * (2 * (n_col - 1 - q) + 1)

    z, y = col // 2, col % 2
    pos = z + y * (n_col - 1 - 2 * z)
    nexts = (to_col(pos + 1), to_col(pos - 1))
    sign = (1, -1)
    mate = x * 2 + (1 - core)

    def tokens(q):
        return pl.ds(pl.multiple_of(to_col(q) * tb, tb), tb)

    def ag(s, d, u, incoming=False, first=False):
        q = pos - sign[d] * s - (sign[d] if incoming else 0)
        cols = pl.ds(d * half + u * sub, sub)
        dst = act_all.at[tokens(q), cols]
        return pltpu.make_async_remote_copy(
            src_ref=own.at[:, cols] if first else dst,
            dst_ref=dst,
            send_sem=ag_send.at[s, d, u],
            recv_sem=ag_recv.at[s, d, u],
            device_id={"row": row, "col": nexts[d]},
            device_id_type=MESH,
        )

    def ag_forward(s):
        for u in range(SUBS):
            for d in range(2):
                ag(s - 1, d, u, incoming=True).wait_recv()
                ag(s, d, u).start()

    def rs(s, i, first=False):
        d = i // PIECES
        q = pos - sign[d] * (1 + s)
        return pltpu.make_async_remote_copy(
            src_ref=part.at[i, tokens(q)] if first else got.at[s - 1, i],
            dst_ref=got.at[s, i],
            send_sem=rs_send.at[s, i],
            recv_sem=rs_recv.at[s, i],
            device_id={"row": row, "col": nexts[d]},
            device_id_type=MESH,
        )

    def shard(r):
        return pl.ds(pl.multiple_of(r * tr, tr), tr)

    def g(k):
        if k == 0:
            src, to = row, mate
        elif k < n_x:
            src, to = row, ((x + k) % n_x) * 2 + core
        else:
            src, to = ((x - (k - n_x + 1) + n_x) % n_x) * 2 + core, mate
        ref = grads.at[shard(src)]
        return pltpu.make_async_remote_copy(
            src_ref=ref, dst_ref=ref, send_sem=g_send.at[k], recv_sem=g_recv.at[k],
            device_id={"row": to, "col": col}, device_id_type=MESH,
        )

    def load(i):
        return pltpu.make_async_copy(
            weight.at[pl.ds(pl.multiple_of(i * piece, piece), piece)], wv.at[i], w_sem.at[i]
        )

    barrier = pltpu.get_barrier_semaphore()
    peers = [{"row": row, "col": nexts[0]}, {"row": row, "col": nexts[1]}, {"row": mate, "col": col}]
    peers += [{"row": ((x + k) % n_x) * 2 + core, "col": col} for k in range(1, n_x)]
    for peer in peers:
        pl.semaphore_signal(barrier, inc=1, device_id=peer, device_id_type=MESH)

    for j in range(width // QB):
        at = slice(j * QB, (j + 1) * QB)
        own[:, at] = (act_v[:, at].astype(jnp.float32) * act_s[:, j:j + 1]).astype(own.dtype)
    for j in range(grad_v.shape[1] // QB):
        at = slice(j * QB, (j + 1) * QB)
        grads[shard(row), at] = (
            grad_v[:, at].astype(jnp.float32) * grad_s[:, j:j + 1]
        ).astype(grads.dtype)

    pl.semaphore_wait(barrier, len(peers))
    for k in range(1, n_x):
        g(k).start()
    for u in range(SUBS):
        for d in range(2):
            ag(0, d, u, first=True).start()
    g(0).start()
    keep = pltpu.make_async_copy(own, act_all.at[tokens(pos)], local_sem.at[0])
    keep.start()
    for i in range(2 * PIECES):
        load((i % 2) * PIECES + i // 2).start()

    def early(s, carry):
        ag_forward(s)
        return carry

    lax.fori_loop(1, n_col - 1 - LATE, early, 0)

    for k in range(1, n_x):
        g(k).wait_recv()
        g(n_x - 1 + k).start()
    g(0).wait_recv()
    for k in range(1, n_x):
        g(n_x - 1 + k).wait_recv()
    store = pltpu.make_async_copy(grads, grad_all, local_sem.at[1])
    store.start()

    def product(k, carry):
        for d in range(2):
            i = d * PIECES + k
            load(i).wait()
            part[i] = lax.dot_general(
                grads[...], wv[i], (((1,), (1,)), ((), ())), preferred_element_type=jnp.float32
            ).astype(part.dtype)
            rs_first(i, d).start()

        @pl.when(k < LATE)
        def _():
            ag_forward(n_col - 1 - LATE + k)

        return carry

    def rs_first(i, d):
        return pltpu.make_async_remote_copy(
            src_ref=part.at[i, tokens(pos - sign[d])],
            dst_ref=got.at[0, i],
            send_sem=rs_send.at[0, i],
            recv_sem=rs_recv.at[0, i],
            device_id={"row": row, "col": nexts[d]},
            device_id_type=MESH,
        )

    lax.fori_loop(0, PIECES, product, 0)

    order = [d * PIECES + k for k in range(PIECES) for d in range(2)]

    def total(s, i):
        q = pos - sign[i // PIECES] * (2 + s)
        return (got[s, i].astype(jnp.float32) + part[i, tokens(q)].astype(jnp.float32)).astype(out.dtype)

    def reduce(s, carry):
        for i in order:
            wait_got(s, i)
            got[s, i] = total(s, i)
            rs(s + 1, i).start()
        return carry

    def wait_got(s, i):
        pltpu.make_async_remote_copy(
            src_ref=got.at[s, i], dst_ref=got.at[s, i],
            send_sem=rs_send.at[s, i], recv_sem=rs_recv.at[s, i],
            device_id={"row": row, "col": nexts[i // PIECES]}, device_id_type=MESH,
        ).wait_recv()

    lax.fori_loop(0, n_col - 2, reduce, 0)
    for i in order:
        wait_got(n_col - 2, i)
        out[:, i * piece:(i + 1) * piece] = total(n_col - 2, i)

    for u in range(SUBS):
        for d in range(2):
            ag(n_col - 2, d, u, incoming=True).wait_recv()
            ag(0, d, u, first=True).wait_send()
    for i in order:
        rs(0, i, first=True).wait_send()

    def drain(s, carry):
        for u in range(SUBS):
            for d in range(2):
                ag(s, d, u).wait_send()
        for i in order:
            rs(s, i).wait_send()
        return carry

    lax.fori_loop(1, n_col - 1, drain, 0)
    for k in range(2 * n_x - 1):
        g(k).wait_send()
    keep.wait()
    store.wait()


def shards(mesh, act_values, act_scales, grad_values, grad_scales, weight):
    n_row, n_col = mesh.shape["row"], mesh.shape["col"]
    tb, width = act_values.shape
    tr, hidden = grad_values.shape
    count = n_row * tr
    piece = width // 2 // PIECES
    dtype = act_values.dtype
    vmem = pl.BlockSpec(memory_space=pltpu.VMEM)
    anywhere = pl.BlockSpec(memory_space=pl.ANY)
    dma = pltpu.SemaphoreType.DMA
    summed, activations, gradients = pl.pallas_call(
        functools.partial(kernel, n_row, n_col),
        out_shape=(
            jax.ShapeDtypeStruct((tb, width), dtype),
            jax.ShapeDtypeStruct((count, width), dtype),
            jax.ShapeDtypeStruct((count, hidden), dtype),
        ),
        in_specs=[vmem, vmem, vmem, vmem, anywhere],
        out_specs=(vmem, anywhere, anywhere),
        scratch_shapes=[
            pltpu.VMEM((tb, width), dtype),
            pltpu.VMEM((count, hidden), dtype),
            pltpu.VMEM((2 * PIECES, piece, hidden), dtype),
            pltpu.VMEM((2 * PIECES, count, piece), dtype),
            pltpu.VMEM((n_col - 1, 2 * PIECES, tb, piece), dtype),
            dma((n_col - 1, 2, SUBS)),
            dma((n_col - 1, 2, SUBS)),
            dma((n_col - 1, 2 * PIECES)),
            dma((n_col - 1, 2 * PIECES)),
            dma((n_row - 1,)),
            dma((n_row - 1,)),
            dma((2 * PIECES,)),
            dma((2,)),
        ],
        compiler_params=pltpu.CompilerParams(
            collective_id=0, has_side_effects=True, vmem_limit_bytes=58 * 1024 * 1024
        ),
        cost_estimate=pl.CostEstimate(
            flops=2 * count * width * hidden,
            bytes_accessed=2 * width * hidden,
            transcendentals=0,
        ),
    )(act_values, act_scales, grad_values, grad_scales, weight)
    weight_grad = lax.dot_general(
        activations, gradients, (((0,), (0,)), ((), ())), preferred_element_type=jnp.float32
    ).astype(jnp.bfloat16)
    return (summed, weight_grad)


def solution(mesh):
    placed = (P("col", "row"), P("col", "row"), P("row", "col"), P("row", "col"), P("row", "col"))
    return jax.shard_map(
        functools.partial(shards, mesh),
        mesh=mesh,
        in_specs=placed,
        out_specs=(P("col", "row"), P("row", "col")),
        check_vma=False,
    )
```

time: 218 us -> 120 us (0.55)
  waiting for transfers between devices: 152 us -> 0 us
  Pallas kernels: 0 us -> 92.8 us
  matrix products: 46.4 us -> 22.6 us
  between operations: 13.8 us -> 0.65 us
  other arithmetic: 3.23 us -> 0 us
    pallas_call x0 -> x1, Pallas kernels: none -> 92.8 us  [shards(): pl.pallas_call(functools.partial(kernel, n_row, n_col), out_shape=(jax.Sh...]
    all_gather x2 -> x0, waiting for transfers between devices: 84.6 us -> none  [the longest x1 51.7 us: shards(): activations = lax.all_gather(act_local, 'col', axis=0, tiled=True)]
    reduce_scatter x1 -> x0, waiting for transfers between devices: 67.8 us -> none  [shards(): lax.psum_scatter(lax.dot_general(gradients, weight, (((1,), (1,)), ((), (...]
    dot_general x1 -> x0, matrix products: 23.8 us -> none  [shards(): lax.dot_general(gradients, weight, (((1,), (1,)), ((), ())), preferred_el...]
    convert_element_type x2 -> x0, other arithmetic: 3.23 us -> none  [dequantize(): return scaled.reshape(height, breadth).astype(jnp.bfloat16)]
  transfers between devices with their start and end apart: 3 -> 0, of which waited for: 3 -> 0; matrix products, arithmetic and copies ran while one was open for 22% -> 0% of each run, Pallas kernels for 0% -> 0%
where the time goes in v1:
time: 120 us
  Pallas kernels  92.8 us (77%)
  matrix products  22.6 us (19%)
  local copies, waits for them, and re-layouts  3.66 us (3%)
    pallas_call x1, Pallas kernels, shards(): pl.pallas_call(functools.partial(kernel, n_row, n_col), out_shape=(jax.Sh...  92.8 us
    dot_general x1, matrix products, shards(): lax.dot_general(activations, gradients, (((0,), (0,)), ((), ())), preferr...  22.6 us
    unnamed x5, local copies, waits for them, and re-layouts  3.66 us

profile of v1, /device:TPU:0, one launch (start us, length us, event | category | flops | bytes accessed | tf_op | source)
XLA Modules:
  0.0 119.7 jit_solution(5809986062645791511)
XLA Ops:
  0.6 1.4 %copy.7.act_s = f32[64,32]{1,0:T(8,128)} copy(f32[64,32]{0,1:T(8,128)} %param.6) | data formatting | bytes 16384 | tf_op args[1]
  2.0 1.4 %copy.8.grad_s = f32[128,28]{1,0:T(8,128)} copy(f32[128,28]{0,1:T(8,128)} %param.8) | data formatting | bytes 28672 | tf_op args[3]
  3.5 92.8 %shard_map.68 = (bf16[64,4096]{1,0:T(8,128)(2,1)}, bf16[512,4096]{1,0:T(8,128)(2,1)}, bf16[512,3584]{1,0:T(8,128)(2,1)}) custom-call(bf16[64,4096]{1,0:T(8,128)(2,1)} %act_v.1, f32[64,32]{1,0:T(8,128)} %copy.7.act_s, bf16[128,3584]{1,0:T(8,128)(2,1)} %grad_v.1, f32[128,28]{1,0:T(8,128)} %copy.8.grad_s, bf16[4096,3584]{1,0:T(8,128)(2,1)} %weight.1), custom_call_target="tpu_custom_call" | custom-call | flops 15032385536 | bytes 29360128 | tf_op jit(solution)/shard_map/pallas_call | solution.py:221
  96.3 0.0 copy-start
  96.3 22.6 %convolution_convert_fusion = bf16[4096,3584]{1,0:T(8,128)(2,1)} fusion(bf16[512,4096]{1,0:T(8,128)(2,1)} %get-tuple-element.6, bf16[512,3584]{1,0:T(8,128)(2,1)} %get-tuple-element.7), kind=kOutput, calls=%fused_computation | convolution fusion | flops 15047065600 | bytes 37224448 | tf_op jit(solution)/shard_map/dot_general | solution.py:254
  118.9 0.0 copy-done
  118.9 0.8 copy.10
Async XLA Ops:
  96.3 22.6 %copy-start = (bf16[64,4096]{1,0:T(8,128)(2,1)S(1)}, bf16[64,4096]{1,0:T(8,128)(2,1)}, u32[]{:S(2)}) copy-start(bf16[64,4096]{1,0:T(8,128)(2,1)} %get-tuple-element.10) | copy-start | bytes 1572868
